TPU v7x, 32 devices: a whole 2x2x4 slice. The times are simulated.
32 devices in a mesh: dp: 8 (over z, x), mlp: 4 (over y, core).
Axes of the slice: x: 2, y: 2, z: 4, core: 2. Of those that a mesh axis runs over, the one named last changes fastest.
Arguments:
- tokens: bfloat16 [2, 6304, 768], P(None, ('dp', 'mlp')), may hold values from -6 to 6
- keep_mask: int32 [2, 6304], P(None, ('dp', 'mlp')), may hold values 0 or 1
- position_index: int32 [197, 197], replicated, may hold values from 0 to 731
- cotangent: bfloat16 [2, 6304, 768], P(None, ('dp', 'mlp')), may hold values from -6 to 6
- first_gain: float32 [768], replicated, may hold values from 0.5 to 1.5
- first_shift: float32 [768], replicated, may hold values from -4 to 4
- inner_weight: bfloat16 [768, 2304], P(('dp', 'mlp')), may hold values from -0.21875 to 0.21875
- query_bias: float32 [768], replicated, may hold values from -6 to 6
- value_bias: float32 [768], replicated, may hold values from -6 to 6
- outer_weight: bfloat16 [768, 768], P(('dp', 'mlp')), may hold values from -0.875 to 0.875
- outer_bias: float32 [768], replicated, may hold values from -4 to 4
- attend_scale: float32 [768], replicated, may hold values from 0.5 to 1.5
- second_gain: float32 [768], replicated, may hold values from 0.5 to 1.5
- second_shift: float32 [768], replicated, may hold values from -4 to 4
- up_weight: bfloat16 [768, 3072], P('dp', 'mlp'), may hold values from -0.21875 to 0.21875
- up_bias: float32 [3072], replicated, may hold values from -6 to 6
- down_weight: bfloat16 [3072, 768], P('mlp', 'dp'), may hold values from -0.109375 to 0.109375
- down_bias: float32 [768], replicated, may hold values from -4 to 4
- feed_scale: float32 [768], replicated, may hold values from 0.5 to 1.5
- position_table: float32 [732, 12], replicated, may hold values from -6 to 6
Outputs:
- result: bfloat16 [2, 6304, 768], P(None, ('dp', 'mlp'))
- gradient_tokens: bfloat16 [2, 6304, 768], P(None, ('dp', 'mlp'))
- gradient_inner: float32 [768, 2304], P(('dp', 'mlp'))
- gradient_outer: float32 [768, 768], P(('dp', 'mlp'))
- gradient_up: float32 [768, 3072], P('dp', 'mlp')
- gradient_down: float32 [3072, 768], P('mlp', 'dp')
- gradient_first_gain: float32 [768], replicated
- gradient_first_shift: float32 [768], replicated
- gradient_query_bias: float32 [768], replicated
- gradient_value_bias: float32 [768], replicated
- gradient_outer_bias: float32 [768], replicated
- gradient_attend_scale: float32 [768], replicated
- gradient_second_gain: float32 [768], replicated
- gradient_second_shift: float32 [768], replicated
- gradient_up_bias: float32 [3072], replicated
- gradient_down_bias: float32 [768], replicated
- gradient_feed_scale: float32 [768], replicated
- gradient_table: float32 [732, 12], replicated
All inputs are finite; a program needn't handle non-finite values. No bound on the sum of `keep_mask` on one device may be relied on, other than what follows from the above.
Results may differ from a plain program's by a relative error of at most 0.014.
Values may be sent and summed in bfloat16 or wider, within the bound.
A program may use at most 192 MiB of HBM per device.

v0:
```python
import jax
import jax.numpy as jnp
from jax import lax
from jax.sharding import PartitionSpec as P

EPS = 1e-06
ROOT_HALF = 0.7071067811865476
DENSITY = 0.3989422804014327


def layer_norm(values, gain, shift):
    mean = jnp.mean(values, -1, keepdims=True)
    centred = values - mean
    variance = jnp.mean(centred * centred, -1, keepdims=True)
    scaled = lax.rsqrt(variance + EPS)
    unit = centred * scaled
    return (unit * gain + shift, unit, scaled)


def norm_back(upstream, unit, scaled, gain):
    inner = upstream * gain
    first = jnp.mean(inner, -1, keepdims=True)
    second = jnp.mean(inner * unit, -1, keepdims=True)
    return (
        scaled * (inner - first - unit * second),
        jnp.sum(upstream * unit, 0),
        jnp.sum(upstream, 0),
    )


def gelu_pair(pre):
    cumul = 0.5 * (1.0 + lax.erf(pre * ROOT_HALF))
    return (pre * cumul, cumul + pre * jnp.exp(-0.5 * pre * pre) * DENSITY)


def fetch(inner_weight, outer_weight, up_weight, down_weight):
    inner_full, outer_full = (
        lax.all_gather(inner_weight, ("dp", "mlp"), axis=0, tiled=True),
        lax.all_gather(outer_weight, ("dp", "mlp"), axis=0, tiled=True),
    )
    up_full, down_full = (
        lax.all_gather(up_weight, "dp", axis=0, tiled=True),
        lax.all_gather(down_weight, "dp", axis=1, tiled=True),
    )
    return (inner_full, outer_full, up_full, down_full)


def contract_rows(left, right):
    return lax.dot_general(
        left, right, (((0,), (0,)), ((), ())), preferred_element_type=jnp.float32
    )


def contract_cols(left, right):
    return lax.dot_general(
        left, right, (((1,), (1,)), ((), ())), preferred_element_type=jnp.float32
    )


def logits_of(query, keys, bias, allowed, factor):
    raw = jnp.einsum("qhd,khd->hqk", query, keys, preferred_element_type=jnp.float32) * factor
    return jnp.where(allowed, raw + bias, -1e30)


def body(
    tokens,
    keep_mask,
    position_index,
    cotangent,
    first_gain,
    first_shift,
    inner_weight,
    query_bias,
    value_bias,
    outer_weight,
    outer_bias,
    attend_scale,
    second_gain,
    second_shift,
    up_weight,
    up_bias,
    down_weight,
    down_bias,
    feed_scale,
    position_table,
):
    micro, rows, width = tokens.shape
    heads = position_table.shape[1]
    head_dim = width // heads
    factor = head_dim ** (-0.5)
    entries = position_table.shape[0]
    columns = up_weight.shape[1]
    col_start = lax.axis_index("mlp") * columns
    up_local = lax.dynamic_slice_in_dim(up_bias, col_start, columns, 0)
    shift_vector = jnp.concatenate([query_bias, jnp.zeros_like(query_bias), value_bias])
    table_by_head = jnp.transpose(position_table)
    bias = table_by_head[:, position_index]
    seen = jnp.arange(rows)
    diagonal = seen[:, None] == seen[None, :]
    flat_index = position_index.reshape(rows * rows)
    zero_width = jnp.zeros((width,), jnp.float32)
    sum_inner = jnp.zeros((width, 3 * width), jnp.float32)
    sum_outer = jnp.zeros((width, width), jnp.float32)
    sum_up = jnp.zeros((width, columns), jnp.float32)
    sum_down = jnp.zeros((columns, width), jnp.float32)
    sum_table_heads = jnp.zeros((heads, entries), jnp.float32)
    sum_up_bias = jnp.zeros((columns,), jnp.float32)
    sum_first_gain = zero_width
    sum_first_shift = zero_width
    sum_query_bias = zero_width
    sum_value_bias = zero_width
    sum_outer_bias = zero_width
    sum_attend_scale = zero_width
    sum_second_gain = zero_width
    sum_second_shift = zero_width
    sum_down_bias = zero_width
    sum_feed_scale = zero_width
    results = []
    input_grads = []
    for index in range(micro):
        inner_full, outer_full, up_full, down_full = fetch(
            inner_weight, outer_weight, up_weight, down_weight
        )
        source = tokens[index].astype(jnp.float32)
        allowed = jnp.logical_or(keep_mask[index][None, :] == 1, diagonal)[None]
        normed_one, unit_one, scaled_one = layer_norm(source, first_gain, first_shift)
        normed_one = normed_one.astype(jnp.bfloat16)
        projected = (
            jnp.dot(normed_one, inner_full, preferred_element_type=jnp.float32) + shift_vector
        ).astype(jnp.bfloat16)
        query = projected[:, :width].reshape(rows, heads, head_dim)
        keys = projected[:, width : 2 * width].reshape(rows, heads, head_dim)
        values = projected[:, 2 * width :].reshape(rows, heads, head_dim)
        logits = logits_of(query, keys, bias, allowed, factor)
        top = jnp.max(logits, -1, keepdims=True)
        expd = jnp.exp(logits - top)
        total = jnp.sum(expd, -1, keepdims=True)
        probs = expd / total
        log_total = top + jnp.log(total)
        mixed = jnp.einsum(
            "hqk,khd->qhd", probs.astype(jnp.bfloat16), values, preferred_element_type=jnp.float32
        )
        mixed = mixed.reshape(rows, width).astype(jnp.bfloat16)
        attend = jnp.dot(mixed, outer_full, preferred_element_type=jnp.float32) + outer_bias
        resid = source + attend_scale * attend
        normed_two, unit_two, scaled_two = layer_norm(resid, second_gain, second_shift)
        normed_two = normed_two.astype(jnp.bfloat16)
        sequence_rows = lax.all_gather(normed_two, "mlp", axis=0, tiled=True)
        pre = jnp.dot(sequence_rows, up_full, preferred_element_type=jnp.float32) + up_local
        active, slope = gelu_pair(pre)
        hidden = active.astype(jnp.bfloat16)
        feed = (
            lax.psum_scatter(
                jnp.dot(hidden, down_full, preferred_element_type=jnp.float32).astype(jnp.bfloat16),
                "mlp",
                scatter_dimension=0,
                tiled=True,
            ).astype(jnp.float32)
            + down_bias
        )
        results.append((resid + feed_scale * feed).astype(jnp.bfloat16))
        inner_full, outer_full, up_full, down_full = fetch(
            inner_weight, outer_weight, up_weight, down_weight
        )
        upstream = cotangent[index].astype(jnp.float32)
        sum_feed_scale = sum_feed_scale + jnp.sum(feed * upstream, 0)
        dfeed = feed_scale * upstream
        sum_down_bias = sum_down_bias + jnp.sum(dfeed, 0)
        upstream_all = lax.all_gather(dfeed.astype(jnp.bfloat16), "mlp", axis=0, tiled=True)
        sum_down = sum_down + contract_rows(hidden, upstream_all)
        dpre = (contract_cols(upstream_all, down_full) * slope).astype(jnp.bfloat16)
        sum_up_bias = sum_up_bias + jnp.sum(dpre.astype(jnp.float32), 0)
        sum_up = sum_up + contract_rows(sequence_rows, dpre)
        dnormed_two = lax.psum_scatter(
            contract_cols(dpre, up_full).astype(jnp.bfloat16),
            "mlp",
            scatter_dimension=0,
            tiled=True,
        ).astype(jnp.float32)
        dresid_norm, part_gain, part_shift = norm_back(
            dnormed_two, unit_two, scaled_two, second_gain
        )
        sum_second_gain = sum_second_gain + part_gain
        sum_second_shift = sum_second_shift + part_shift
        dresid = upstream + dresid_norm
        sum_attend_scale = sum_attend_scale + jnp.sum(attend * dresid, 0)
        dattend = attend_scale * dresid
        sum_outer_bias = sum_outer_bias + jnp.sum(dattend, 0)
        dattend_low = dattend.astype(jnp.bfloat16)
        sum_outer = sum_outer + contract_rows(mixed, dattend_low)
        dmixed = (
            contract_cols(dattend_low, outer_full)
            .astype(jnp.bfloat16)
            .reshape(rows, heads, head_dim)
        )
        logits = logits_of(query, keys, bias, allowed, factor)
        probs = jnp.exp(logits - log_total)
        dvalues = jnp.einsum(
            "hqk,qhd->khd", probs.astype(jnp.bfloat16), dmixed, preferred_element_type=jnp.float32
        )
        dprobs = jnp.einsum("qhd,khd->hqk", dmixed, values, preferred_element_type=jnp.float32)
        dlogits = probs * (dprobs - jnp.sum(dprobs * probs, -1, keepdims=True))
        sum_table_heads = sum_table_heads.at[:, flat_index].add(dlogits.reshape(heads, rows * rows))
        dlogits_low = dlogits.astype(jnp.bfloat16)
        dquery = (
            jnp.einsum("hqk,khd->qhd", dlogits_low, keys, preferred_element_type=jnp.float32)
            * factor
        )
        dkeys = (
            jnp.einsum("hqk,qhd->khd", dlogits_low, query, preferred_element_type=jnp.float32)
            * factor
        )
        dprojected = jnp.concatenate(
            [dquery.reshape(rows, width), dkeys.reshape(rows, width), dvalues.reshape(rows, width)],
            axis=1,
        ).astype(jnp.bfloat16)
        sum_query_bias = sum_query_bias + jnp.sum(dprojected[:, :width].astype(jnp.float32), 0)
        sum_value_bias = sum_value_bias + jnp.sum(dprojected[:, 2 * width :].astype(jnp.float32), 0)
        sum_inner = sum_inner + contract_rows(normed_one, dprojected)
        dnormed_one = contract_cols(dprojected, inner_full)
        dsource_norm, part_gain, part_shift = norm_back(
            dnormed_one, unit_one, scaled_one, first_gain
        )
        sum_first_gain = sum_first_gain + part_gain
        sum_first_shift = sum_first_shift + part_shift
        input_grads.append((dresid + dsource_norm).astype(jnp.bfloat16))
    sum_table = jnp.transpose(sum_table_heads)
    gradient_inner, gradient_outer = (
        lax.psum_scatter(sum_inner, ("dp", "mlp"), scatter_dimension=0, tiled=True),
        lax.psum_scatter(sum_outer, ("dp", "mlp"), scatter_dimension=0, tiled=True),
    )
    gradient_up, gradient_down = (
        lax.psum_scatter(sum_up, "dp", scatter_dimension=0, tiled=True),
        lax.psum_scatter(sum_down, "dp", scatter_dimension=1, tiled=True),
    )
    up_bias_full = lax.dynamic_update_slice_in_dim(
        jnp.zeros((up_bias.shape[0],), jnp.float32), sum_up_bias, col_start, 0
    )
    summed = lax.psum(
        (
            sum_first_gain,
            sum_first_shift,
            sum_query_bias,
            sum_value_bias,
            sum_outer_bias,
            sum_attend_scale,
            sum_second_gain,
            sum_second_shift,
            up_bias_full,
            sum_down_bias,
            sum_feed_scale,
            sum_table,
        ),
        ("dp", "mlp"),
    )
    return (
        jnp.stack(results),
        jnp.stack(input_grads),
        gradient_inner,
        gradient_outer,
        gradient_up,
        gradient_down,
        summed[0],
        summed[1],
        summed[2],
        summed[3],
        summed[4],
        summed[5],
        summed[6],
        summed[7],
        summed[8],
        summed[9],
        summed[10],
        summed[11],
    )


def solution(mesh):
    placed = (
        P(None, ("dp", "mlp"), None),
        P(None, ("dp", "mlp")),
        P(),
        P(None, ("dp", "mlp"), None),
        P(),
        P(),
        P(("dp", "mlp"), None),
        P(),
        P(),
        P(("dp", "mlp"), None),
        P(),
        P(),
        P(),
        P(),
        P("dp", "mlp"),
        P(),
        P("mlp", "dp"),
        P(),
        P(),
        P(),
    )
    return jax.shard_map(
        body,
        mesh=mesh,
        in_specs=placed,
        out_specs=(
            P(None, ("dp", "mlp"), None),
            P(None, ("dp", "mlp"), None),
            P(("dp", "mlp"), None),
            P(("dp", "mlp"), None),
            P("dp", "mlp"),
            P("mlp", "dp"),
            P(),
            P(),
            P(),
            P(),
            P(),
            P(),
            P(),
            P(),
            P(),
            P(),
            P(),
            P(),
        ),
        check_vma=False,
    )
```

profile of v0, /device:TPU:0, one launch (start us, length us, event | category | flops | bytes accessed | tf_op | source)
XLA Modules:
  0.0 1434.0 jit_solution(9241634660880689768)
XLA Ops:
  8.7 2.4 fusion.121
  14.9 128.7 %gather_fusion = f32[38809,12]{1,0:T(8,128)} fusion(f32[12,732]{0,1:T(8,128)S(1)} %bitcast.219, s32[38912]{0:T(1024)S(1)} %pad_clamp_fusion), kind=kCustom, calls=%fused_computation | custom fusion | bytes 3880900 | tf_op jit(solution)/shard_map/gather | solution.py:97
  143.5 11.1 copy.105
  154.6 2.8 reshape.322
  157.4 2.3 copy.106
  160.3 3.3 fusion.5
  164.5 1.9 copy.109
  166.4 1.9 copy.110
  168.3 1.9 copy.111
  170.2 3.0 fusion.4
  176.2 2.0 copy.103
  186.5 1.9 convolution_add_fusion.6
  199.2 2.7 reshape.350
  201.9 2.7 reshape.348
  204.7 7.7 all-gather.23.cloned.1.call-done
  212.4 2.6 reshape.346
  215.0 16.5 %all-gather.21.cloned.1.call-done = bf16[4,197,768]{2,1,0:T(8,128)(2,1)} async-done(((bf16[1,197,768]{2,1,0:T(8,128)(2,1)}), bf16[4,197,768]{2,1,0:T(8,128)(2,1)}) %all-gather.21.cloned.1.call-update) | async-done | bytes 1210384 | tf_op jit(solution)/shard_map/all_gather | solution.py:148
  231.6 2.6 reshape.344
  234.2 40.6 %all-gather.17.cloned.1.call-done = bf16[768,768]{1,0:T(8,128)(2,1)} async-done(((bf16[96,768]{1,0:T(8,128)(2,1)}), bf16[768,768]{1,0:T(8,128)(2,1)}) %all-gather.17.cloned.1.call-update) | async-done | bytes 1179664 | tf_op jit(solution)/shard_map/all_gather | solution.py:42
  274.9 2.9 fusion.125
  279.2 3.5 multiply_convert_fusion.1
  282.8 34.1 %all-gather.19.cloned.1.call-done = bf16[768,768]{0,1:T(8,128)(2,1)} async-done(((bf16[768,96]{0,1:T(8,128)(2,1)}), bf16[768,768]{0,1:T(8,128)(2,1)}) %all-gather.19.cloned.1.call-update) | async-done | bytes 1179664 | tf_op jit(solution)/shard_map/all_gather | solution.py:43
  316.9 4.0 convolution_convert_fusion.2
  320.9 2.3 convolution_convert_fusion.3
  323.2 2.3 convert_reduce_fusion
  325.5 2.2 convolution_convert_fusion
  328.4 2.2 convert_reduce_fusion.1
  331.7 2.2 convolution_convert_fusion.1
  333.9 46.6 %fusion.114 = (bf16[200,768]{1,0:T(8,128)(2,1)}, bf16[200,768]{1,0:T(8,128)(2,1)}, bf16[200,768]{1,0:T(8,128)(2,1)}, bf16[200,768]{1,0:T(8,128)(2,1)}) fusion(bf16[788,768]{1,0:T(8,128)(2,1)} %convolution_convert_fusion.2, bf16[788,768]{1,0:T(8,128)(2,1)} %convolution_convert_fusion.3, bf16[788,768]{1,0:T(8,128)(2,1)} %convolution_convert_fusion, ...), kind=kCustom, calls=%all-reduce-scatter.4 | all-reduce-scatter fusion | flops 2457601 | bytes 6070784
  381.3 1.9 collective-permute-start.2
  383.9 3.2 collective-permute-start.1
  387.9 1.9 collective-permute-start.3
  390.6 1.9 collective-permute-start
  393.0 4.0 concatenate.17
  399.7 4.0 concatenate.16
  403.7 4.0 concatenate.15
  407.8 3.4 fusion.82
  413.3 1.9 copy.119
  415.2 3.2 convolution_convert_fusion.4
  422.9 4.0 concatenate.14
  426.9 3.0 multiply_reduce_fusion.3
  438.9 1.9 fusion.105
  440.8 3.4 copy.123
  444.2 2.2 copy.125
  448.8 4.7 fusion.74
  453.9 2.9 reshape.326
  456.8 9.7 copy.124
  466.6 2.8 reshape.334
  469.3 9.7 copy.126
  479.0 3.8 fusion.90
  490.0 207.4 %scatter_custom_fusion = f32[12,732]{0,1:T(8,128)S(1)} fusion(s32[38809]{0:T(1024)S(1)} %bitcast.254, f32[38809,12]{1,0:T(8,128)} %copy.124, f32[]{:T(128)} %constant.17.clone.1), kind=kCustom, calls=%fused_computation.189 | custom fusion | flops 465708 | bytes 35648 | tf_op jit(solution)/shard_map/scatter-add | solution.py:203
  697.5 207.6 %scatter_fusion = f32[12,732]{0,1:T(8,128)S(1)} fusion(f32[12,732]{0,1:T(8,128)S(1)} %scatter_custom_fusion, s32[38809]{0:T(1024)S(1)} %bitcast.255, f32[38809,12]{1,0:T(8,128)} %copy.126), kind=kCustom, calls=%fused_computation.2 | custom fusion | flops 465708 | bytes 5743732 | tf_op jit(solution)/shard_map/scatter-add | solution.py:203
  905.9 3.6 convolution_add_fusion.3
  909.8 3.2 fusion.126
  913.1 3.0 convolution_add_fusion.5
  916.2 3.3 fusion.127
  919.5 2.9 convolution_add_fusion.4
  923.6 2.4 fusion.91
  926.0 4.3 convolution_add_fusion
  934.3 102.6 %all-reduce.12.cloned.1.call-done = (f32[768]{0:T(1024)}, f32[768]{0:T(1024)}, f32[768]{0:T(1024)}, f32[768]{0:T(1024)}, f32[768]{0:T(1024)}, /*index=5*/f32[768...) async-done(((f32[768]{0:T(1024)}, f32[768]{0:T(1024)}, f32[768]{0:T(1024)}, ...) | async-done | bytes 78160 | tf_op jit(solution)/shard_map/psum | solution.py:239
  1038.7 104.1 %reduce-scatter.15.cloned.1.call-done = f32[24,768]{1,0:T(8,128)} async-done(((f32[768,768]{1,0:T(8,128)}), f32[24,768]{1,0:T(8,128)}) %reduce-scatter.15.cloned.1.call-update) | async-done | bytes 73744 | tf_op jit(solution)/shard_map/reduce_scatter | solution.py:230
  1142.8 72.6 %reduce-scatter.17.cloned.1.call-done = f32[96,768]{1,0:T(8,128)} async-done(((f32[768,768]{1,0:T(8,128)}), f32[96,768]{1,0:T(8,128)}) %reduce-scatter.17.cloned.1.call-update) | async-done | bytes 294928 | tf_op jit(solution)/shard_map/reduce_scatter | solution.py:233
  1215.4 72.4 %reduce-scatter.19.cloned.1.call-done = f32[768,96]{0,1:T(8,128)} async-done(((f32[768,768]{0,1:T(8,128)}), f32[768,96]{0,1:T(8,128)}) %reduce-scatter.19.cloned.1.call-update) | async-done | bytes 294928 | tf_op jit(solution)/shard_map/reduce_scatter | solution.py:234
  1287.8 125.4 %reduce-scatter.13.cloned.1.call-done = f32[24,2304]{1,0:T(8,128)} async-done(((f32[768,2304]{1,0:T(8,128)}), f32[24,2304]{1,0:T(8,128)}) %reduce-scatter.13.cloned.1.call-update) | async-done | bytes 221200 | tf_op jit(solution)/shard_map/reduce_scatter | solution.py:229
  (344 shorter events, 84.4 us)
Async XLA Ops:
  7.2 3.9 copy-start.70
  7.2 153.0 %all-gather.13.cloned.1.call-start = ((), (), s32[]{:S(2)}) async-start(), calls=%async_computation.4 | async-start | bytes 3649536 | tf_op jit(solution)/shard_map/all_gather | solution.py:38
  7.9 178.5 %all-gather.15.cloned.1.call-start = ((), (), s32[]{:S(2)}) async-start(), calls=%async_computation.5 | async-start | bytes 1216512 | tf_op jit(solution)/shard_map/all_gather | solution.py:39
  8.7 4.3 copy-start.36
  8.7 190.5 %all-gather.27.cloned.1.call-start = ((), (), s32[]{:S(2)}) async-start(), calls=%async_computation.15 | async-start | bytes 1536000 | tf_op jit(solution)/shard_map/all_gather | solution.py:169
  12.3 189.6 %all-gather.25.cloned.1.call-start = ((), (), s32[]{:S(2)}) async-start(), calls=%async_computation.14 | async-start | bytes 1536000 | tf_op jit(solution)/shard_map/all_gather | solution.py:169
  12.9 199.5 %all-gather.23.cloned.1.call-start = ((), (), s32[]{:S(2)}) async-start(), calls=%async_computation.13 | async-start | bytes 1536000 | tf_op jit(solution)/shard_map/all_gather | solution.py:148
  14.0 156.2 %copy-start.17 = (bf16[1,197,768]{2,1,0:T(8,128)(2,1)}, bf16[1,197,768]{2,1,0:T(8,128)(2,1)S(1)}, u32[]{:S(2)}) copy-start(bf16[1,197,768]{2,1,0:T(8,128)(2,1)S(1)} %get-tuple-element.179) | copy-start | bytes 907780
  14.3 146.0 %copy-start.72 = (f32[197]{0:T(256)}, f32[197]{0:T(256)S(1)}, u32[]{:S(2)}) copy-start(f32[197]{0:T(256)S(1)} %add_rsqrt_fusion.1) | copy-start | bytes 2368
  159.7 18.5 %copy-start.6 = (f32[197,197,12]{0,1,2:T(8,128)}, f32[197,197,12]{0,1,2:T(8,128)S(1)}, u32[]{:S(2)}) copy-start(f32[197,197,12]{0,1,2:T(8,128)S(1)} %copy.106) | copy-start | bytes 5588500
  159.8 10.4 copy-start.78
  160.0 10.2 copy-start.88
  176.2 6.6 copy-start.24
  185.1 3.4 copy-start.58
  189.9 4.0 copy-start.74
  190.1 3.8 copy-start.76
  190.4 3.6 copy-start.83
  191.8 39.7 %all-gather.21.cloned.1.call-start = ((), (), s32[]{:S(2)}) async-start(), calls=%async_computation.12 | async-start | bytes 1536000 | tf_op jit(solution)/shard_map/all_gather | solution.py:148
  192.4 82.4 %all-gather.17.cloned.1.call-start = ((), (), s32[]{:S(2)}) async-start(), calls=%async_computation.6 | async-start | bytes 1327104 | tf_op jit(solution)/shard_map/all_gather | solution.py:42
  193.2 123.7 %all-gather.19.cloned.1.call-start = ((), (), s32[]{:S(2)}) async-start(), calls=%async_computation.7 | async-start | bytes 1327104 | tf_op jit(solution)/shard_map/all_gather | solution.py:43
  194.0 842.9 %all-reduce.12.cloned.1.call-start = ((), (), s32[]{:S(2)}) async-start(), calls=%async_computation.16 | async-start | bytes 860160 | tf_op jit(solution)/shard_map/psum | solution.py:239
  199.1 5.5 copy-start.60
  199.1 5.5 copy-start.64
  199.1 5.5 copy-start.62
  199.2 5.5 copy-start.66
  274.8 4.4 copy-start.52
  274.9 4.4 copy-start.94
  316.9 4.0 copy-start.96
  316.9 4.0 copy-start.101
  333.9 63.1 %copy-start.77 = (f32[197]{0:T(256)S(1)}, f32[197]{0:T(256)}, u32[]{:S(2)}) copy-start(f32[197]{0:T(256)} %copy-done.76) | copy-start | bytes 2368
  333.9 63.1 %copy-start.87 = (f32[197]{0:T(256)S(1)}, f32[197]{0:T(256)}, u32[]{:S(2)}) copy-start(f32[197]{0:T(256)} %copy-done.86) | copy-start | bytes 2368
  380.5 27.3 %copy-start.71 = (f32[768]{0:T(1024)S(1)}, f32[768]{0:T(1024)}, u32[]{:S(2)}) copy-start(f32[768]{0:T(1024)} %param.38) | copy-start | bytes 9220
  380.5 27.3 %copy-start.75 = (f32[197]{0:T(256)S(1)}, f32[197]{0:T(256)}, u32[]{:S(2)}) copy-start(f32[197]{0:T(256)} %copy-done.74) | copy-start | bytes 2368
  380.5 27.3 %copy-start.81 = (f32[768]{0:T(1024)S(1)}, f32[768]{0:T(1024)}, u32[]{:S(2)}) copy-start(f32[768]{0:T(1024)} %param.37) | copy-start | bytes 9220
  380.5 27.3 %copy-start.84 = (f32[197]{0:T(256)S(1)}, f32[197]{0:T(256)}, u32[]{:S(2)}) copy-start(f32[197]{0:T(256)} %copy-done.83) | copy-start | bytes 2368
  381.3 18.4 %collective-permute-start.2 = (bf16[9,768]{1,0:T(8,128)(2,1)S(1)}, bf16[9,768]{1,0:T(8,128)(2,1)}, u32[]{:S(2)}, u32[]{:S(2)}) collective-permute-start(bf16[9,768]{1,0:T(8,128)(2,1)S(1)} %slice.62), channel_id=1, source_target_pairs={{0,1},{1,2},{2,3},{4,5},{5,6},{6,7},{8,9},{9,10},{10,11},{12,13},{... | collective-permute-start | bytes 41480
  383.9 19.8 %collective-permute-start.1 = (bf16[9,768]{1,0:T(8,128)(2,1)S(1)}, bf16[9,768]{1,0:T(8,128)(2,1)}, u32[]{:S(2)}, u32[]{:S(2)}) collective-permute-start(bf16[9,768]{1,0:T(8,128)(2,1)S(1)} %slice.61), channel_id=1, source_target_pairs={{0,1},{1,2},{2,3},{4,5},{5,6},{6,7},{8,9},{9,10},{10,11},{12,13},{... | collective-permute-start | bytes 41480
  387.9 5.1 collective-permute-start.3
  390.6 32.3 %collective-permute-start = (bf16[9,768]{1,0:T(8,128)(2,1)S(1)}, bf16[9,768]{1,0:T(8,128)(2,1)}, u32[]{:S(2)}, u32[]{:S(2)}) collective-permute-start(bf16[9,768]{1,0:T(8,128)(2,1)S(1)} %slice.60), channel_id=1, source_target_pairs={{0,1},{1,2},{2,3},{4,5},{5,6},{6,7},{8,9},{9,10},{10,11},{12,13},{... | collective-permute-start | bytes 41480
  393.0 18.2 %copy-start.69 = (f32[3072]{0:T(1024)}, f32[3072]{0:T(1024)S(1)}, u32[]{:S(2)}) copy-start(f32[3072]{0:T(1024)S(1)} %add_dynamic-update-slice_fusion) | copy-start | bytes 36868
  407.7 4.3 copy-start.9
  421.7 5.2 copy-start.82
  421.7 5.2 copy-start.85
  426.9 3.8 copy-start.10
  440.8 3.4 copy-start.4
  444.2 4.5 copy-start.19
  444.2 4.5 copy-start.79
  444.2 4.5 copy-start.89
  448.8 4.7 copy-start.32
  448.8 4.9 copy-start.30
  479.0 3.8 copy-start.14
  479.0 3.8 copy-start.55
  479.0 3.8 copy-start.73
  482.8 7.3 copy-start.34
  482.8 7.3 copy-start.54
  697.5 208.5 %copy-start.16 = (f32[197,768]{1,0:T(8,128)S(1)}, f32[197,768]{1,0:T(8,128)}, u32[]{:S(2)}) copy-start(f32[197,768]{1,0:T(8,128)} %copy-done.15) | copy-start | bytes 1815556
  697.5 208.5 %copy-start.43 = (bf16[12,64,197]{2,1,0:T(8,128)(2,1)S(1)}, bf16[12,64,197]{2,1,0:T(8,128)(2,1)}, u32[]{:S(2)}) copy-start(bf16[12,64,197]{2,1,0:T(8,128)(2,1)} %convolution_convert_fusion.6) | copy-start | bytes 907780
  905.9 236.9 %reduce-scatter.15.cloned.1.call-start = ((), (), s32[]{:S(2)}) async-start(), calls=%async_computation.9 | async-start | bytes 2433024 | tf_op jit(solution)/shard_map/reduce_scatter | solution.py:230
  909.5 3.5 copy-start.51
  909.5 305.9 %reduce-scatter.17.cloned.1.call-start = ((), (), s32[]{:S(2)}) async-start(), calls=%async_computation.10 | async-start | bytes 2654208 | tf_op jit(solution)/shard_map/reduce_scatter | solution.py:233
  916.1 3.4 copy-start.49
  916.1 371.7 %reduce-scatter.19.cloned.1.call-start = ((), (), s32[]{:S(2)}) async-start(), calls=%async_computation.11 | async-start | bytes 2654208 | tf_op jit(solution)/shard_map/reduce_scatter | solution.py:234
  922.5 3.5 copy-start.31
  922.5 490.8 %reduce-scatter.13.cloned.1.call-start = ((), (), s32[]{:S(2)}) async-start(), calls=%async_computation.8 | async-start | bytes 7299072 | tf_op jit(solution)/shard_map/reduce_scatter | solution.py:229
  (58 other events, 115.9 us)
Sparse Core Ops, SparseCore 0:
  10.9 62.8 all-gather.12
  76.7 52.8 all-gather.14
  131.2 16.6 all-gather.26
  149.3 17.7 all-gather.24
  192.0 20.3 all-gather.22
  213.8 17.7 all-gather.20
  233.8 41.0 all-gather.16
  277.0 39.8 all-gather.18
  906.0 130.8 all-reduce.11
  1042.6 100.1 reduce-scatter.14
  1147.3 68.0 reduce-scatter.16
  1219.7 68.0 reduce-scatter.18
  1295.0 118.1 reduce-scatter.12
where the time goes:
time: 1440 us; the launch traced here: 1430 us
  waiting for transfers between devices  580 us (40%)
  other arithmetic  441 us (31%)
  local copies, waits for them, and re-layouts  257 us (18%)
  matrix products  83.5 us (6%)
  blocking collectives  46.6 us (3%)
  between operations  16.1 us (1%)
    scatter-add x2, other arithmetic, body(): sum_table_heads.at[:, flat_index].add(dlogits.reshape(heads, rows * rows))  415 us
    gather x4, local copies, waits for them, and re-layouts, body(): bias = table_by_head[:, position_index]  145 us
    reduce_scatter x1, waiting for transfers between devices, body(): lax.psum_scatter(sum_inner, ('dp', 'mlp'), scatter_dimension=0, tiled=True)  125 us
    reduce_scatter x1, waiting for transfers between devices, body(): lax.psum_scatter(sum_outer, ('dp', 'mlp'), scatter_dimension=0, tiled=True)  104 us
    psum x1, waiting for transfers between devices, body(): lax.psum((sum_first_gain, sum_first_shift, sum_query_bias, sum_value_bias...  103 us
    reduce_scatter x1, waiting for transfers between devices, body(): lax.psum_scatter(sum_up, 'dp', scatter_dimension=0, tiled=True)  72.6 us
    reduce_scatter x1, waiting for transfers between devices, body(): lax.psum_scatter(sum_down, 'dp', scatter_dimension=1, tiled=True)  72.4 us
    unnamed x238, local copies, waits for them, and re-layouts  60.9 us
  transfers between devices with their start and end apart: 17, of which 9 were waited for; matrix products, arithmetic and copies ran while one was open for 18% of the time, Pallas kernels for 0%

commit v1 on v0

--- a/solution.py
+++ b/solution.py
@@ -237,21 +237,24 @@
         jnp.zeros((up_bias.shape[0],), jnp.float32), sum_up_bias, col_start, 0
     )
     summed = lax.psum(
-        (
-            sum_first_gain,
-            sum_first_shift,
-            sum_query_bias,
-            sum_value_bias,
-            sum_outer_bias,
-            sum_attend_scale,
-            sum_second_gain,
-            sum_second_shift,
-            up_bias_full,
-            sum_down_bias,
-            sum_feed_scale,
-            sum_table,
+        lax.psum(
+            (
+                sum_first_gain,
+                sum_first_shift,
+                sum_query_bias,
+                sum_value_bias,
+                sum_outer_bias,
+                sum_attend_scale,
+                sum_second_gain,
+                sum_second_shift,
+                up_bias_full,
+                sum_down_bias,
+                sum_feed_scale,
+                sum_table,
+            ),
+            "mlp",
         ),
-        ("dp", "mlp"),
+        "dp",
     )
     return (
         jnp.stack(results),

time: 1440 us -> 1420 us (0.986)
  waiting for transfers between devices: 580 us -> 559 us
    psum x1, waiting for transfers between devices: 103 us -> 29.2 us  [body(): lax.psum((sum_first_gain, sum_first_shift, sum_query_bias, sum_value_bias...]
    psum x0 -> x1, waiting for transfers between devices: none -> 54.2 us  [body(): lax.psum(lax.psum((sum_first_gain, sum_first_shift, sum_query_bias, sum_v...]
    unnamed x238 -> x236, local copies, waits for them, and re-layouts: 60.9 us -> 60.9 us
  transfers between devices with their start and end apart: 17 -> 18, of which waited for: 9 -> 10; matrix products, arithmetic and copies ran while one was open for 18% -> 19% of each run, Pallas kernels for 0% -> 0%
where the time goes in v1:
time: 1420 us; the launch traced here: 1410 us
  waiting for transfers between devices  559 us (39%)
  other arithmetic  441 us (31%)
  local copies, waits for them, and re-layouts  258 us (18%)
  matrix products  83.5 us (6%)
  blocking collectives  46.6 us (3%)
  between operations  16.1 us (1%)
    scatter-add x2, other arithmetic, body(): sum_table_heads.at[:, flat_index].add(dlogits.reshape(heads, rows * rows))  415 us
    gather x4, local copies, waits for them, and re-layouts, body(): bias = table_by_head[:, position_index]  146 us
    reduce_scatter x1, waiting for transfers between devices, body(): lax.psum_scatter(sum_inner, ('dp', 'mlp'), scatter_dimension=0, tiled=True)  125 us
    reduce_scatter x1, waiting for transfers between devices, body(): lax.psum_scatter(sum_outer, ('dp', 'mlp'), scatter_dimension=0, tiled=True)  103 us
    reduce_scatter x1, waiting for transfers between devices, body(): lax.psum_scatter(sum_down, 'dp', scatter_dimension=1, tiled=True)  72.6 us
    reduce_scatter x1, waiting for transfers between devices, body(): lax.psum_scatter(sum_up, 'dp', scatter_dimension=0, tiled=True)  72.4 us
    unnamed x236, local copies, waits for them, and re-layouts  60.9 us
    psum x1, waiting for transfers between devices, body(): lax.psum(lax.psum((sum_first_gain, sum_first_shift, sum_query_bias, sum_v...  54.2 us
  transfers between devices with their start and end apart: 18, of which 10 were waited for; matrix products, arithmetic and copies ran while one was open for 19% of the time, Pallas kernels for 0%

profile of v1, /device:TPU:0, one launch (start us, length us, event | category | flops | bytes accessed | tf_op | source)
XLA Modules:
  0.0 1414.2 jit_solution(4817378885646267253)
XLA Ops:
  8.7 2.4 fusion.121
  14.8 129.6 %gather_fusion = f32[38809,12]{1,0:T(8,128)} fusion(f32[12,732]{0,1:T(8,128)S(1)} %bitcast.219, s32[38912]{0:T(1024)S(1)} %pad_clamp_fusion), kind=kCustom, calls=%fused_computation | custom fusion | bytes 3880900 | tf_op jit(solution)/shard_map/gather | solution.py:97
  144.5 11.1 copy.105
  155.5 2.8 reshape.322
  158.3 2.3 copy.106
  161.2 3.3 fusion.5
  165.4 1.9 copy.109
  169.2 1.9 copy.111
  171.1 3.0 fusion.4
  177.1 2.0 copy.103
  187.4 1.9 convolution_add_fusion.6
  200.1 2.7 reshape.350
  202.8 2.7 reshape.348
  205.6 7.8 all-gather.23.cloned.1.call-done
  213.4 2.6 reshape.346
  216.1 16.5 %all-gather.21.cloned.1.call-done = bf16[4,197,768]{2,1,0:T(8,128)(2,1)} async-done(((bf16[1,197,768]{2,1,0:T(8,128)(2,1)}), bf16[4,197,768]{2,1,0:T(8,128)(2,1)}) %all-gather.21.cloned.1.call-update) | async-done | bytes 1210384 | tf_op jit(solution)/shard_map/all_gather | solution.py:148
  232.6 2.7 reshape.344
  235.3 40.6 %all-gather.17.cloned.1.call-done = bf16[768,768]{1,0:T(8,128)(2,1)} async-done(((bf16[96,768]{1,0:T(8,128)(2,1)}), bf16[768,768]{1,0:T(8,128)(2,1)}) %all-gather.17.cloned.1.call-update) | async-done | bytes 1179664 | tf_op jit(solution)/shard_map/all_gather | solution.py:42
  275.9 2.9 fusion.125
  280.3 3.5 multiply_convert_fusion.1
  283.8 34.1 %all-gather.19.cloned.1.call-done = bf16[768,768]{0,1:T(8,128)(2,1)} async-done(((bf16[768,96]{0,1:T(8,128)(2,1)}), bf16[768,768]{0,1:T(8,128)(2,1)}) %all-gather.19.cloned.1.call-update) | async-done | bytes 1179664 | tf_op jit(solution)/shard_map/all_gather | solution.py:43
  317.9 4.0 convolution_convert_fusion.2
  322.0 2.3 convolution_convert_fusion.3
  324.3 2.2 convert_reduce_fusion
  326.6 2.2 convolution_convert_fusion
  329.5 2.2 convert_reduce_fusion.1
  332.7 2.2 convolution_convert_fusion.1
  335.0 46.6 %fusion.114 = (bf16[200,768]{1,0:T(8,128)(2,1)}, bf16[200,768]{1,0:T(8,128)(2,1)}, bf16[200,768]{1,0:T(8,128)(2,1)}, bf16[200,768]{1,0:T(8,128)(2,1)}) fusion(bf16[788,768]{1,0:T(8,128)(2,1)} %convolution_convert_fusion.2, bf16[788,768]{1,0:T(8,128)(2,1)} %convolution_convert_fusion.3, bf16[788,768]{1,0:T(8,128)(2,1)} %convolution_convert_fusion, ...), kind=kCustom, calls=%all-reduce-scatter.4 | all-reduce-scatter fusion | flops 2457601 | bytes 6070784
  382.4 1.9 collective-permute-start.2
  385.0 3.2 collective-permute-start.1
  389.0 1.9 collective-permute-start.3
  391.6 1.9 collective-permute-start
  394.1 4.0 concatenate.17
  400.8 4.0 concatenate.16
  404.8 4.0 concatenate.15
  408.8 3.4 fusion.82
  414.3 1.9 copy.119
  416.2 3.2 convolution_convert_fusion.4
  423.9 4.0 concatenate.14
  427.9 3.0 multiply_reduce_fusion.3
  440.0 3.4 copy.123
  443.5 2.2 copy.125
  448.0 4.7 fusion.74
  453.2 2.8 reshape.326
  455.9 9.9 copy.124
  465.8 2.8 reshape.334
  468.6 9.7 copy.126
  478.3 3.8 fusion.90
  489.3 207.4 %scatter_custom_fusion = f32[12,732]{0,1:T(8,128)S(1)} fusion(s32[38809]{0:T(1024)S(1)} %bitcast.254, f32[38809,12]{1,0:T(8,128)} %copy.124, f32[]{:T(128)} %constant.17.clone.1), kind=kCustom, calls=%fused_computation.189 | custom fusion | flops 465708 | bytes 35648 | tf_op jit(solution)/shard_map/scatter-add | solution.py:203
  696.7 207.6 %scatter_fusion = f32[12,732]{0,1:T(8,128)S(1)} fusion(f32[12,732]{0,1:T(8,128)S(1)} %scatter_custom_fusion, s32[38809]{0:T(1024)S(1)} %bitcast.255, f32[38809,12]{1,0:T(8,128)} %copy.126), kind=kCustom, calls=%fused_computation.2 | custom fusion | flops 465708 | bytes 5743732 | tf_op jit(solution)/shard_map/scatter-add | solution.py:203
  905.1 2.0 fusion.105
  907.1 29.2 %all-reduce.16.cloned.1.call-done = (f32[768]{0:T(1024)}, f32[768]{0:T(1024)}, f32[768]{0:T(1024)}, f32[768]{0:T(1024)}, f32[768]{0:T(1024)}, /*index=5*/f32[768...) async-done(((f32[768]{0:T(1024)}, f32[768]{0:T(1024)}, f32[768]{0:T(1024)}, ...) | async-done | bytes 78160 | tf_op jit(solution)/shard_map/psum | solution.py:240
  936.3 3.6 convolution_add_fusion.3
  940.1 3.2 fusion.126
  943.3 2.9 convolution_add_fusion.5
  946.6 3.2 fusion.127
  949.8 2.9 convolution_add_fusion.4
  953.8 2.4 fusion.91
  956.2 4.3 convolution_add_fusion
  964.5 54.2 %all-reduce.14.cloned.1.call-done = (f32[768]{0:T(1024)}, f32[768]{0:T(1024)}, f32[768]{0:T(1024)}, f32[768]{0:T(1024)}, f32[768]{0:T(1024)}, /*index=5*/f32[768...) async-done(((f32[768]{0:T(1024)}, f32[768]{0:T(1024)}, f32[768]{0:T(1024)}, ...) | async-done | bytes 78160 | tf_op jit(solution)/shard_map/psum | solution.py:239
  1020.5 102.6 %reduce-scatter.15.cloned.1.call-done = f32[24,768]{1,0:T(8,128)} async-done(((f32[768,768]{1,0:T(8,128)}), f32[24,768]{1,0:T(8,128)}) %reduce-scatter.15.cloned.1.call-update) | async-done | bytes 73744 | tf_op jit(solution)/shard_map/reduce_scatter | solution.py:230
  1123.1 72.4 %reduce-scatter.17.cloned.1.call-done = f32[96,768]{1,0:T(8,128)} async-done(((f32[768,768]{1,0:T(8,128)}), f32[96,768]{1,0:T(8,128)}) %reduce-scatter.17.cloned.1.call-update) | async-done | bytes 294928 | tf_op jit(solution)/shard_map/reduce_scatter | solution.py:233
  1195.5 72.6 %reduce-scatter.19.cloned.1.call-done = f32[768,96]{0,1:T(8,128)} async-done(((f32[768,768]{0,1:T(8,128)}), f32[768,96]{0,1:T(8,128)}) %reduce-scatter.19.cloned.1.call-update) | async-done | bytes 294928 | tf_op jit(solution)/shard_map/reduce_scatter | solution.py:234
  1268.2 125.3 %reduce-scatter.13.cloned.1.call-done = f32[24,2304]{1,0:T(8,128)} async-done(((f32[768,2304]{1,0:T(8,128)}), f32[24,2304]{1,0:T(8,128)}) %reduce-scatter.13.cloned.1.call-update) | async-done | bytes 221200 | tf_op jit(solution)/shard_map/reduce_scatter | solution.py:229
  (345 shorter events, 86.3 us)
Async XLA Ops:
  7.2 3.9 copy-start.69
  7.2 153.9 %all-gather.13.cloned.1.call-start = ((), (), s32[]{:S(2)}) async-start(), calls=%async_computation.4 | async-start | bytes 3649536 | tf_op jit(solution)/shard_map/all_gather | solution.py:38
  7.9 179.4 %all-gather.15.cloned.1.call-start = ((), (), s32[]{:S(2)}) async-start(), calls=%async_computation.5 | async-start | bytes 1216512 | tf_op jit(solution)/shard_map/all_gather | solution.py:39
  8.7 4.2 copy-start.35
  8.7 191.4 %all-gather.27.cloned.1.call-start = ((), (), s32[]{:S(2)}) async-start(), calls=%async_computation.15 | async-start | bytes 1536000 | tf_op jit(solution)/shard_map/all_gather | solution.py:169
  12.3 190.5 %all-gather.25.cloned.1.call-start = ((), (), s32[]{:S(2)}) async-start(), calls=%async_computation.14 | async-start | bytes 1536000 | tf_op jit(solution)/shard_map/all_gather | solution.py:169
  12.9 200.5 %all-gather.23.cloned.1.call-start = ((), (), s32[]{:S(2)}) async-start(), calls=%async_computation.13 | async-start | bytes 1536000 | tf_op jit(solution)/shard_map/all_gather | solution.py:148
  14.0 157.2 %copy-start.16 = (bf16[1,197,768]{2,1,0:T(8,128)(2,1)}, bf16[1,197,768]{2,1,0:T(8,128)(2,1)S(1)}, u32[]{:S(2)}) copy-start(bf16[1,197,768]{2,1,0:T(8,128)(2,1)S(1)} %get-tuple-element.191) | copy-start | bytes 907780
  14.2 146.9 %copy-start.71 = (f32[197]{0:T(256)}, f32[197]{0:T(256)S(1)}, u32[]{:S(2)}) copy-start(f32[197]{0:T(256)S(1)} %add_rsqrt_fusion.1) | copy-start | bytes 2368
  160.6 18.5 %copy-start.6 = (f32[197,197,12]{0,1,2:T(8,128)}, f32[197,197,12]{0,1,2:T(8,128)S(1)}, u32[]{:S(2)}) copy-start(f32[197,197,12]{0,1,2:T(8,128)S(1)} %copy.106) | copy-start | bytes 5588500
  160.7 10.5 copy-start.77
  160.9 10.2 copy-start.87
  177.1 6.6 copy-start.23
  190.8 4.0 copy-start.73
  191.1 3.8 copy-start.75
  191.3 3.6 copy-start.82
  192.8 39.8 %all-gather.21.cloned.1.call-start = ((), (), s32[]{:S(2)}) async-start(), calls=%async_computation.12 | async-start | bytes 1536000 | tf_op jit(solution)/shard_map/all_gather | solution.py:148
  193.3 82.5 %all-gather.17.cloned.1.call-start = ((), (), s32[]{:S(2)}) async-start(), calls=%async_computation.6 | async-start | bytes 1327104 | tf_op jit(solution)/shard_map/all_gather | solution.py:42
  194.1 123.8 %all-gather.19.cloned.1.call-start = ((), (), s32[]{:S(2)}) async-start(), calls=%async_computation.7 | async-start | bytes 1327104 | tf_op jit(solution)/shard_map/all_gather | solution.py:43
  194.9 741.4 %all-reduce.16.cloned.1.call-start = ((), (), s32[]{:S(2)}) async-start(), calls=%async_computation.17 | async-start | bytes 860160 | tf_op jit(solution)/shard_map/psum | solution.py:240
  200.0 5.5 copy-start.59
  200.1 5.5 copy-start.63
  200.1 5.5 copy-start.61
  200.1 5.5 copy-start.65
  275.9 4.4 copy-start.51
  275.9 4.4 copy-start.93
  317.9 4.0 copy-start.95
  317.9 4.0 copy-start.100
  334.9 63.1 %copy-start.76 = (f32[197]{0:T(256)S(1)}, f32[197]{0:T(256)}, u32[]{:S(2)}) copy-start(f32[197]{0:T(256)} %copy-done.75) | copy-start | bytes 2368
  335.0 63.1 %copy-start.86 = (f32[197]{0:T(256)S(1)}, f32[197]{0:T(256)}, u32[]{:S(2)}) copy-start(f32[197]{0:T(256)} %copy-done.85) | copy-start | bytes 2368
  381.5 27.2 %copy-start.70 = (f32[768]{0:T(1024)S(1)}, f32[768]{0:T(1024)}, u32[]{:S(2)}) copy-start(f32[768]{0:T(1024)} %param.38) | copy-start | bytes 9220
  381.6 27.2 %copy-start.74 = (f32[197]{0:T(256)S(1)}, f32[197]{0:T(256)}, u32[]{:S(2)}) copy-start(f32[197]{0:T(256)} %copy-done.73) | copy-start | bytes 2368
  381.6 27.2 %copy-start.80 = (f32[768]{0:T(1024)S(1)}, f32[768]{0:T(1024)}, u32[]{:S(2)}) copy-start(f32[768]{0:T(1024)} %param.37) | copy-start | bytes 9220
  381.6 27.2 %copy-start.83 = (f32[197]{0:T(256)S(1)}, f32[197]{0:T(256)}, u32[]{:S(2)}) copy-start(f32[197]{0:T(256)} %copy-done.82) | copy-start | bytes 2368
  382.4 18.4 %collective-permute-start.2 = (bf16[9,768]{1,0:T(8,128)(2,1)S(1)}, bf16[9,768]{1,0:T(8,128)(2,1)}, u32[]{:S(2)}, u32[]{:S(2)}) collective-permute-start(bf16[9,768]{1,0:T(8,128)(2,1)S(1)} %slice.62), channel_id=1, source_target_pairs={{0,1},{1,2},{2,3},{4,5},{5,6},{6,7},{8,9},{9,10},{10,11},{12,13},{... | collective-permute-start | bytes 41480
  385.0 19.8 %collective-permute-start.1 = (bf16[9,768]{1,0:T(8,128)(2,1)S(1)}, bf16[9,768]{1,0:T(8,128)(2,1)}, u32[]{:S(2)}, u32[]{:S(2)}) collective-permute-start(bf16[9,768]{1,0:T(8,128)(2,1)S(1)} %slice.61), channel_id=1, source_target_pairs={{0,1},{1,2},{2,3},{4,5},{5,6},{6,7},{8,9},{9,10},{10,11},{12,13},{... | collective-permute-start | bytes 41480
  389.0 5.1 collective-permute-start.3
  391.6 32.3 %collective-permute-start = (bf16[9,768]{1,0:T(8,128)(2,1)S(1)}, bf16[9,768]{1,0:T(8,128)(2,1)}, u32[]{:S(2)}, u32[]{:S(2)}) collective-permute-start(bf16[9,768]{1,0:T(8,128)(2,1)S(1)} %slice.60), channel_id=1, source_target_pairs={{0,1},{1,2},{2,3},{4,5},{5,6},{6,7},{8,9},{9,10},{10,11},{12,13},{... | collective-permute-start | bytes 41480
  394.0 18.2 %copy-start.68 = (f32[3072]{0:T(1024)}, f32[3072]{0:T(1024)S(1)}, u32[]{:S(2)}) copy-start(f32[3072]{0:T(1024)S(1)} %add_dynamic-update-slice_fusion) | copy-start | bytes 36868
  408.8 4.3 copy-start.9
  422.7 5.2 copy-start.81
  422.7 5.2 copy-start.84
  427.9 3.9 copy-start.10
  440.0 3.4 copy-start.4
  443.4 4.6 copy-start.18
  443.4 4.6 copy-start.78
  443.5 4.6 copy-start.88
  448.0 4.8 copy-start.31
  448.0 4.9 copy-start.29
  478.3 3.8 copy-start.13
  478.3 3.8 copy-start.54
  478.3 3.8 copy-start.72
  482.0 214.7 %copy-start.33 = (f32[197,768]{1,0:T(8,128)}, f32[197,768]{1,0:T(8,128)S(1)}, u32[]{:S(2)}) copy-start(f32[197,768]{1,0:T(8,128)S(1)} %fusion.90) | copy-start | bytes 1815556
  482.0 7.2 copy-start.53
  696.7 208.4 %copy-start.37 = (bf16[12,64,197]{2,1,0:T(8,128)(2,1)S(1)}, bf16[12,64,197]{2,1,0:T(8,128)(2,1)}, u32[]{:S(2)}) copy-start(bf16[12,64,197]{2,1,0:T(8,128)(2,1)} %convolution_convert_fusion.7) | copy-start | bytes 907780
  904.3 32.0 %copy-start.15 = (f32[197,768]{1,0:T(8,128)S(1)}, f32[197,768]{1,0:T(8,128)}, u32[]{:S(2)}) copy-start(f32[197,768]{1,0:T(8,128)} %copy-done.14) | copy-start | bytes 1815556
  904.3 32.0 %copy-start.42 = (bf16[12,64,197]{2,1,0:T(8,128)(2,1)S(1)}, bf16[12,64,197]{2,1,0:T(8,128)(2,1)}, u32[]{:S(2)}) copy-start(bf16[12,64,197]{2,1,0:T(8,128)(2,1)} %convolution_convert_fusion.6) | copy-start | bytes 907780
  905.1 113.6 %all-reduce.14.cloned.1.call-start = ((), (), s32[]{:S(2)}) async-start(), calls=%async_computation.16 | async-start | bytes 860160 | tf_op jit(solution)/shard_map/psum | solution.py:239
  936.3 186.8 %reduce-scatter.15.cloned.1.call-start = ((), (), s32[]{:S(2)}) async-start(), calls=%async_computation.9 | async-start | bytes 2433024 | tf_op jit(solution)/shard_map/reduce_scatter | solution.py:230
  940.0 255.5 %reduce-scatter.17.cloned.1.call-start = ((), (), s32[]{:S(2)}) async-start(), calls=%async_computation.10 | async-start | bytes 2654208 | tf_op jit(solution)/shard_map/reduce_scatter | solution.py:233
  946.3 321.9 %reduce-scatter.19.cloned.1.call-start = ((), (), s32[]{:S(2)}) async-start(), calls=%async_computation.11 | async-start | bytes 2654208 | tf_op jit(solution)/shard_map/reduce_scatter | solution.py:234
  952.7 3.5 copy-start.30
  952.7 3.5 copy-start.32
  952.7 440.7 %reduce-scatter.13.cloned.1.call-start = ((), (), s32[]{:S(2)}) async-start(), calls=%async_computation.8 | async-start | bytes 7299072 | tf_op jit(solution)/shard_map/reduce_scatter | solution.py:229
  (58 other events, 119.9 us)
Sparse Core Ops, SparseCore 0:
  10.9 62.8 all-gather.12
  76.7 52.8 all-gather.14
  131.2 16.6 all-gather.26
  149.3 17.7 all-gather.24
  192.9 20.4 all-gather.22
  214.8 17.7 all-gather.20
  234.8 41.0 all-gather.16
  278.1 39.8 all-gather.18
  905.2 31.0 all-reduce.15
  941.9 76.7 all-reduce.13
  1024.6 98.4 reduce-scatter.14
  1127.4 68.0 reduce-scatter.16
  1200.0 68.0 reduce-scatter.18
  1275.2 118.2 reduce-scatter.12
